TPU v7x, 256 devices: a whole 4x4x8 slice. The times are simulated.
256 devices in a mesh: tm: 32 (over z, y), clip: 8 (over x, core).
Axes of the slice: x: 4, y: 4, z: 8, core: 2. Of those that a mesh axis runs over, the one named last changes fastest.
Arguments:
- block_input: bfloat16 [8, 128, 16, 16, 256], P('clip', 'tm'), may hold values from -6 to 6
- pre_act: bfloat16 [8, 128, 16, 16, 512], P('clip', 'tm'), may hold values from -6 to 6
- time_out: bfloat16 [8, 128, 16, 16, 512], P('clip', 'tm'), may hold values from -6 to 6
- w_space: bfloat16 [256, 3, 3, 512], replicated, may hold values from -0.125 to 0.125
- w_time: bfloat16 [512, 3, 512], replicated, may hold values from -0.15625 to 0.15625
- proj: bfloat16 [512, 18], replicated, may hold values from -0.25 to 0.25
- codes: int32 [8, 128, 16, 16], P('clip', 'tm'), may hold values from 0 to 262143
- cotan: bfloat16 [8, 128, 16, 16, 18], P('clip', 'tm'), may hold values from -6 to 6
- lengths: int32 [8], replicated, may hold values from 1 to 128
Outputs:
- grad_input: bfloat16 [8, 128, 256, 256], P('clip', None, 'tm')
- grad_space: float32 [256, 3, 3, 512], P('tm')
- grad_time: float32 [512, 3, 512], P('tm')
- grad_proj: float32 [512, 18], P('tm')
All inputs are finite; a program needn't handle non-finite values.
Results may differ from a plain program's by a relative error of at most 0.025.
Values may be sent and summed in bfloat16 or wider, within the bound.
A program may use at most 64 MiB of HBM per device.

v0:
```python
import math
import jax
import jax.numpy as jnp
from jax import lax
from jax.sharding import PartitionSpec as P

commit_weight = 0.25


def from_behind(shard, axis, by):
    devices = lax.axis_size(axis)
    pairs = [(i, i + by) for i in range(devices) if 0 <= i + by < devices]
    return lax.ppermute(shard, axis, pairs)


def shift_space(values, down, right):
    side_len = values.shape[-2]
    padded = jnp.pad(values, ((0, 0), (1, 1), (1, 1), (0, 0)))
    return padded[:, 1 + down : 1 + down + side_len, 1 + right : 1 + right + side_len, :]


def silu_slope(pre):
    sigma = jax.nn.sigmoid(pre)
    return sigma * (1.0 + pre * (1.0 - sigma))


def sign_targets(flat_codes, latent):
    powers = (2 ** jnp.arange(latent)).astype(jnp.int32)
    bits = flat_codes[:, None] // powers[None, :] % 2
    return 2.0 * bits.astype(jnp.float32) - 1.0


def per_device(block_input, pre_act, time_out, w_space, w_time, proj, codes, cotan, lengths):
    clip_x = block_input[0]
    clip_pre = pre_act[0]
    frames_dev, side_len, _, cin = clip_x.shape
    cmid = clip_pre.shape[-1]
    latent = proj.shape[1]
    positions = side_len * side_len
    rows = frames_dev * positions
    slab_count = lax.axis_size("tm")
    group_count = lax.axis_size("clip")
    scale = 1.0 / math.sqrt(group_count * slab_count * rows)
    clip_len = lax.dynamic_index_in_dim(lengths, lax.axis_index("clip"), 0, keepdims=False)
    frame_ids = lax.axis_index("tm") * frames_dev + jnp.arange(frames_dev)
    live = (frame_ids < clip_len).astype(jnp.float32)
    live_rows = jnp.repeat(live, positions)[:, None]
    t_rows = time_out[0].reshape(rows, cmid)
    latent_z = jnp.dot(t_rows, proj, preferred_element_type=jnp.float32)
    targets = sign_targets(codes[0].reshape(rows), latent)
    grad_z = (
        live_rows
        * (
            cotan[0].reshape(rows, latent).astype(jnp.float32)
            + 2.0 * commit_weight * (latent_z - targets)
        )
    ).astype(jnp.bfloat16)
    proj_part = jnp.dot(t_rows.T, grad_z, preferred_element_type=jnp.float32)
    grad_t = jnp.dot(grad_z, proj.T, preferred_element_type=jnp.float32).astype(jnp.bfloat16)
    grad_t = grad_t.reshape(frames_dev, positions, cmid)
    grad_t_rows = grad_t.reshape(rows, cmid)
    next_frames = from_behind(grad_t[:2], "tm", -1)
    t_ext = jnp.concatenate([grad_t, next_frames], axis=0)
    act = (
        jax.nn.silu(clip_pre.astype(jnp.float32))
        .astype(jnp.bfloat16)
        .reshape(frames_dev, positions, cmid)
    )
    grad_act = jnp.zeros((rows, cmid), jnp.float32)
    for lag in range(3):
        ahead = t_ext[lag : lag + frames_dev].reshape(rows, cmid)
        grad_act = grad_act + jnp.dot(
            ahead, w_time[:, lag, :].T, preferred_element_type=jnp.float32
        )
    time_terms = []
    prev_frames = from_behind(act[frames_dev - 2 :], "tm", 1)
    a_ext = jnp.concatenate([prev_frames, act], axis=0)
    for lag in range(3):
        behind = a_ext[2 - lag : 2 - lag + frames_dev].reshape(rows, cmid)
        time_terms.append(jnp.dot(behind.T, grad_t_rows, preferred_element_type=jnp.float32))
    time_part = jnp.stack(time_terms, axis=1)
    grad_pre = (
        grad_act.reshape(frames_dev, side_len, side_len, cmid)
        * silu_slope(clip_pre.astype(jnp.float32))
    ).astype(jnp.bfloat16)
    pre_rows = grad_pre.reshape(rows, cmid)
    grad_x = jnp.zeros((frames_dev, side_len, side_len, cin), jnp.float32)
    space_rows = []
    for row_tap in range(3):
        row_terms = []
        for col_tap in range(3):
            moved = shift_space(clip_x, row_tap - 1, col_tap - 1).reshape(rows, cin)
            row_terms.append(jnp.dot(moved.T, pre_rows, preferred_element_type=jnp.float32))
            back = jnp.dot(
                pre_rows, w_space[:, row_tap, col_tap, :].T, preferred_element_type=jnp.float32
            )
            grad_x = grad_x + shift_space(
                back.reshape(frames_dev, side_len, side_len, cin), 1 - row_tap, 1 - col_tap
            )
        space_rows.append(jnp.stack(row_terms, axis=1))
    space_part = jnp.stack(space_rows, axis=1)
    grad_cells = grad_x.astype(jnp.bfloat16).reshape(1, frames_dev, positions, cin)
    grad_input = lax.all_to_all(grad_cells, "tm", split_axis=2, concat_axis=1, tiled=True)
    space_part = space_part * scale
    time_part = time_part * scale
    proj_part = proj_part * scale
    summed = (
        lax.psum(space_part.astype(jnp.bfloat16), "clip").astype(jnp.float32),
        lax.psum(time_part.astype(jnp.bfloat16), "clip").astype(jnp.float32),
        lax.psum(proj_part.astype(jnp.bfloat16), "clip").astype(jnp.float32),
    )
    owned = (
        lax.psum_scatter(
            summed[0].astype(jnp.bfloat16), "tm", scatter_dimension=0, tiled=True
        ).astype(jnp.float32),
        lax.psum_scatter(
            summed[1].astype(jnp.bfloat16), "tm", scatter_dimension=0, tiled=True
        ).astype(jnp.float32),
        lax.psum_scatter(
            summed[2].astype(jnp.bfloat16), "tm", scatter_dimension=0, tiled=True
        ).astype(jnp.float32),
    )
    return (grad_input, owned[0], owned[1], owned[2])


def solution(mesh):
    placed = (
        P("clip", "tm", None, None, None),
        P("clip", "tm", None, None, None),
        P("clip", "tm", None, None, None),
        P(),
        P(),
        P(),
        P("clip", "tm", None, None),
        P("clip", "tm", None, None, None),
        P(),
    )
    return jax.shard_map(
        per_device,
        mesh=mesh,
        in_specs=placed,
        out_specs=(
            P("clip", None, "tm", None),
            P("tm", None, None, None),
            P("tm", None, None),
            P("tm", None),
        ),
        check_vma=False,
    )
```

profile of v0, /device:TPU:1, one launch (start us, length us, event | category | flops | bytes accessed | tf_op | source)
XLA Modules:
  0.0 757.8 jit_solution(11394494174237194665)
XLA Ops:
  7.3 1.3 dynamic_slice.4
  8.6 0.6 compare_convert_fusion
  9.3 0.8 broadcast_in_dim_reshape_squeeze.3
  10.1 1.0 bitcast_convert_fusion
  11.1 0.2 copy.44
  11.3 2.0 fusion.18
  13.4 0.5 convolution_convert_fusion
  13.9 1.3 collective-permute-start
  15.2 0.7 fusion.30
  15.9 11.3 %collective-permute-done = bf16[2,256,512]{2,1,0:T(8,128)(2,1)S(1)} collective-permute-done((bf16[2,256,512]{2,1,0:T(8,128)(2,1)S(1)}, bf16[2,256,512]{2,1,0:T(8,128)(2,1)S(1)}, u32[]{:S(2)}, u32[]{:S(2)}) %collective-permute-start) | collective-permute-done | bytes 524320 | tf_op jit(solution)/shard_map/ppermute | solution.py:13
  27.3 0.2 pad_maximum_fusion.1
  27.5 0.7 fusion.28
  28.2 0.5 copy-done.1
  28.7 2.5 fusion.9
  31.2 2.2 add_divide_fusion
  33.4 0.5 convolution_bitcast_fusion.10
  33.9 0.5 convolution_bitcast_fusion.11
  34.3 0.5 convolution_bitcast_fusion.9
  34.8 0.5 convolution_bitcast_fusion.6
  35.3 0.5 convolution_bitcast_fusion.8
  35.8 0.5 convolution_bitcast_fusion.3
  36.2 0.5 convolution_bitcast_fusion.4
  36.7 0.5 convolution_bitcast_fusion.5
  37.2 0.5 convolution_bitcast_fusion.7
  37.7 0.1 maximum_bitcast_fusion
  38.0 0.7 fusion
  38.7 3.7 copy.45
  42.4 7.4 reshape.147
  49.8 0.2 fusion.20
  50.1 0.8 copy.47
  50.9 0.2 reduce-scatter.8.cloned.1.call-start
  51.1 1.7 convert_bitcast_fusion
  52.8 0.6 multiply_convert_fusion
  53.4 0.3 fusion.26
  53.7 5.4 collective-permute-start.1
  59.1 0.7 convolution_bitcast_fusion.2
  59.8 2.4 fusion.35
  62.3 6.5 collective-permute-done.1
  68.7 0.2 fusion.21
  68.9 0.7 convolution_bitcast_fusion
  69.6 0.7 convolution_bitcast_fusion.1
  70.4 1.6 fusion.1
  72.0 1.6 fusion.37
  73.6 0.2 copy-done.5
  73.8 0.5 fusion.39
  74.2 0.5 fusion.41
  74.7 0.5 fusion.44
  75.2 0.5 fusion.46
  75.7 0.5 fusion.48
  76.1 0.5 fusion.50
  76.6 0.3 copy-done.4
  76.9 0.8 fusion.14
  77.7 1.2 copy.22
  78.9 14.4 %all-to-all-start = ((bf16[1,4,256,256]{3,1,0,2:T(4,128)(2,1)}), bf16[1,4,256,256]{3,1,0,2:T(4,128)(2,1)S(1)}, u32[]{:S(2)}, u32[]{:S(2)}) async-start(bf16[1,4,256,256]{3,1,0,2:T(4,128)(2,1)} %copy.22), calls=%async_computation | async-start | bytes 1048576 | tf_op jit(solution)/shard_map/all_to_all | solution.py:103
  93.4 177.9 %reduce-scatter.10.cloned.1.call-done = bf16[8,4608]{1,0:T(8,128)(2,1)} async-done(((bf16[256,4608]{1,0:T(8,128)(2,1)}), bf16[8,4608]{1,0:T(8,128)(2,1)}) %reduce-scatter.10.cloned.1.call-update) | async-done | bytes 73744
  271.4 194.6 %reduce-scatter.12.cloned.1.call-done = bf16[16,18]{1,0:T(8,128)(2,1)} async-done(((bf16[512,18]{1,0:T(8,128)(2,1)}), bf16[16,18]{1,0:T(8,128)(2,1)}) %reduce-scatter.12.cloned.1.call-update) | async-done | bytes 592
  465.9 0.8 copy.48
  466.7 0.9 copy.23
  467.6 216.4 %reduce-scatter.8.cloned.1.call-done = bf16[16,3,512]{2,0,1:T(8,128)(2,1)} async-done(((bf16[512,3,512]{2,0,1:T(8,128)(2,1)}), bf16[16,3,512]{2,0,1:T(8,128)(2,1)}) %reduce-scatter.8.cloned.1.call-update) | async-done | bytes 49168 | tf_op jit(solution)/shard_map/reduce_scatter | solution.py:116
  684.0 27.6 %all-reduce.9 = (bf16[16,18]{0,1:T(8,128)(2,1)S(1)}, bf16[16,3,512]{2,0,1:T(8,128)(2,1)S(1)}) all-reduce(bf16[16,18]{0,1:T(8,128)(2,1)S(1)} %copy.48, bf16[16,3,512]{2,0,1:T(8,128)(2,1)} %reduce-scatter.8.cloned.1.call-done), channel_id=1, replica_groups=mesh['tm'=32,'clip'=8] {'clip'}, use_global_device_ids=true, to_apply=%region_4.5 | all-reduce | flops 24864 | bytes 99456 | tf_op jit(solution)/shard_map/psum | solution.py:110
  711.5 0.6 convert_element_type.124
  712.2 0.7 copy.25
  712.9 36.9 %all-reduce.12.cloned.1.call-done = bf16[8,3,3,512]{3,0,2,1:T(8,128)(2,1)} async-done(((bf16[8,3,3,512]{3,0,2,1:T(8,128)(2,1)}), bf16[8,3,3,512]{3,0,2,1:T(8,128)(2,1)}) %all-reduce.12.cloned.1.call-update) | async-done | bytes 73744 | tf_op jit(solution)/shard_map/psum | solution.py:108
  749.7 1.6 convert_element_type.117
  (32 shorter events, 0.6 us)
Async XLA Ops:
  7.2 4.2 copy-start
  7.2 6.2 copy-start.8
  7.2 264.1 %reduce-scatter.10.cloned.1.call-start = ((), (), s32[]{:S(2)}) async-start(), calls=%async_computation.6 | async-start | bytes 2433024
  11.3 3.9 copy-start.6
  13.9 13.4 %collective-permute-start = (bf16[2,256,512]{2,1,0:T(8,128)(2,1)S(1)}, bf16[2,256,512]{2,1,0:T(8,128)(2,1)S(1)}, u32[]{:S(2)}, u32[]{:S(2)}) collective-permute-start(bf16[2,256,512]{2,1,0:T(8,128)(2,1)S(1)} %bitcast.259), channel_id=1, source_target_pairs={{8,0},{16,8},{24,16},{32,24},{40,32},{48,40},{56,48},{64,56},{72,6... | collective-permute-start | bytes 1572872 | tf_op jit(solution)/shard_map/ppermute | solution.py:13
  27.5 1.2 copy-start.1
  31.2 2.2 copy-start.7
  49.8 416.2 %reduce-scatter.12.cloned.1.call-start = ((), (), s32[]{:S(2)}) async-start(), calls=%async_computation.7 | async-start | bytes 135168
  50.9 633.1 %reduce-scatter.8.cloned.1.call-start = ((), (), s32[]{:S(2)}) async-start(), calls=%async_computation.5 | async-start | bytes 1622016 | tf_op jit(solution)/shard_map/reduce_scatter | solution.py:116
  51.1 1.7 copy-start.2
  51.1 2.3 copy-start.3
  52.8 6.3 copy-start.9
  53.7 15.0 %collective-permute-start.1 = (bf16[2,256,512]{2,1,0:T(8,128)(2,1)S(1)}, bf16[2,256,512]{2,1,0:T(8,128)(2,1)S(1)}, u32[]{:S(2)}, u32[]{:S(2)}) collective-permute-start(bf16[2,256,512]{2,1,0:T(8,128)(2,1)S(1)} %bitcast.257), channel_id=1, source_target_pairs={{0,8},{8,16},{16,24},{24,32},{32,40},{40,48},{48,56},{56,64},{64,7... | collective-permute-start | bytes 1572872 | tf_op jit(solution)/shard_map/ppermute | solution.py:13
  72.0 1.7 copy-start.5
  75.7 1.2 copy-start.4
  78.9 387.8 %all-to-all-start = ((bf16[1,4,256,256]{3,1,0,2:T(4,128)(2,1)}), bf16[1,4,256,256]{3,1,0,2:T(4,128)(2,1)S(1)}, u32[]{:S(2)}, u32[]{:S(2)}) async-start(bf16[1,4,256,256]{3,1,0,2:T(4,128)(2,1)} %copy.22), calls=%async_computation | async-start | bytes 1048576 | tf_op jit(solution)/shard_map/all_to_all | solution.py:103
  93.4 656.3 %all-reduce.12.cloned.1.call-start = ((), (), s32[]{:S(2)}) async-start(), calls=%async_computation.4 | async-start | bytes 147456 | tf_op jit(solution)/shard_map/psum | solution.py:108
Sparse Core Ops, SparseCore 0:
  49.9 221.4 reduce-scatter.9
  275.5 190.3 reduce-scatter.11
  470.2 213.6 reduce-scatter.7
  686.3 63.3 all-reduce.11
where the time goes:
time: 759 us; the launch traced here: 758 us
  waiting for transfers between devices  644 us (85%)
  blocking collectives  27.6 us (4%)
  starting transfers between devices  21.4 us (3%)
  matrix products  20.7 us (3%)
  local copies, waits for them, and re-layouts  18.8 us (2%)
  between operations  14.2 us (2%)
  other arithmetic  11.6 us (2%)
    unnamed x6, waiting for transfers between devices  373 us
    reduce_scatter x1, waiting for transfers between devices, per_device(): lax.psum_scatter(summed[1].astype(jnp.bfloat16), 'tm', scatter_dimension=...  216 us
    psum x1, waiting for transfers between devices, per_device(): lax.psum(space_part.astype(jnp.bfloat16), 'clip').astype(jnp.float32)  36.9 us
    psum x1, blocking collectives, per_device(): lax.psum(proj_part.astype(jnp.bfloat16), 'clip').astype(jnp.float32)  27.6 us
    ppermute x2, waiting for transfers between devices, from_behind(): return lax.ppermute(shard, axis, pairs)  17.8 us
  transfers between devices with their start and end apart: 7, of which 6 were waited for; matrix products, arithmetic and copies ran while one was open for 3% of the time, Pallas kernels for 0%

commit v1 on v0

--- a/solution.py
+++ b/solution.py
@@ -105,7 +105,9 @@
     time_part = time_part * scale
     proj_part = proj_part * scale
     summed = (
-        lax.psum(space_part.astype(jnp.bfloat16), "clip").astype(jnp.float32),
+        jnp.sum(lax.all_gather(space_part.astype(jnp.bfloat16), "clip"), axis=0).astype(
+            jnp.float32
+        ),
         lax.psum(time_part.astype(jnp.bfloat16), "clip").astype(jnp.float32),
         lax.psum(proj_part.astype(jnp.bfloat16), "clip").astype(jnp.float32),
     )

time: 759 us -> 693 us (0.913)
  waiting for transfers between devices: 644 us -> 564 us
  other arithmetic: 11.6 us -> 24.9 us
    unnamed x6, waiting for transfers between devices: 373 us -> 245 us
    all_gather x0 -> x1, waiting for transfers between devices: none -> 82.9 us  [per_device(): lax.all_gather(space_part.astype(jnp.bfloat16), 'clip')]
    psum x1 -> x0, waiting for transfers between devices: 36.9 us -> none  [per_device(): lax.psum(space_part.astype(jnp.bfloat16), 'clip').astype(jnp.float32)]
    reduce_sum x0 -> x1, other arithmetic: none -> 11.9 us  [per_device(): jnp.sum(lax.all_gather(space_part.astype(jnp.bfloat16), 'clip'), axis=0)]
    unnamed x27 -> x25, local copies, waits for them, and re-layouts: 14.3 us -> 15.9 us
  transfers between devices with their start and end apart: 7 -> 7, of which waited for: 6 -> 6; matrix products, arithmetic and copies ran while one was open for 3% -> 6% of each run, Pallas kernels for 0% -> 0%
where the time goes in v1:
time: 693 us; the launch traced here: 688 us
  waiting for transfers between devices  564 us (81%)
  blocking collectives  27.5 us (4%)
  other arithmetic  24.9 us (4%)
  local copies, waits for them, and re-layouts  20.4 us (3%)
  matrix products  18.6 us (3%)
  starting transfers between devices  16.7 us (2%)
  between operations  16 us (2%)
    unnamed x6, waiting for transfers between devices  245 us
    reduce_scatter x1, waiting for transfers between devices, per_device(): lax.psum_scatter(summed[1].astype(jnp.bfloat16), 'tm', scatter_dimension=...  217 us
    all_gather x1, waiting for transfers between devices, per_device(): lax.all_gather(space_part.astype(jnp.bfloat16), 'clip')  82.9 us
    psum x1, blocking collectives, per_device(): lax.psum(proj_part.astype(jnp.bfloat16), 'clip').astype(jnp.float32)  27.5 us
    ppermute x2, waiting for transfers between devices, from_behind(): return lax.ppermute(shard, axis, pairs)  19.4 us
    unnamed x25, local copies, waits for them, and re-layouts  15.9 us
  transfers between devices with their start and end apart: 7, of which 6 were waited for; matrix products, arithmetic and copies ran while one was open for 6% of the time, Pallas kernels for 0%

profile of v1, /device:TPU:1, one launch (start us, length us, event | category | flops | bytes accessed | tf_op | source)
XLA Modules:
  0.0 688.0 jit_solution(15908798638807486840)
XLA Ops:
  8.1 1.3 dynamic_slice.4
  9.4 0.6 compare_convert_fusion
  10.1 0.8 broadcast_in_dim_reshape_squeeze.3
  11.0 1.0 bitcast_convert_fusion
  12.0 0.2 copy.44
  12.2 2.0 fusion.18
  14.2 0.5 convolution_convert_fusion
  14.7 1.3 collective-permute-start
  16.0 0.7 fusion.30
  16.8 11.4 %collective-permute-done = bf16[2,256,512]{2,1,0:T(8,128)(2,1)S(1)} collective-permute-done((bf16[2,256,512]{2,1,0:T(8,128)(2,1)S(1)}, bf16[2,256,512]{2,1,0:T(8,128)(2,1)S(1)}, u32[]{:S(2)}, u32[]{:S(2)}) %collective-permute-start) | collective-permute-done | bytes 524320 | tf_op jit(solution)/shard_map/ppermute | solution.py:13
  28.1 0.2 pad_maximum_fusion.1
  28.3 0.7 fusion.28
  29.1 0.5 copy-done.1
  29.5 2.3 fusion.9
  31.9 2.3 add_divide_fusion
  34.1 0.5 convolution_bitcast_fusion.10
  34.6 0.5 convolution_bitcast_fusion.11
  35.1 0.5 convolution_bitcast_fusion.9
  35.6 0.5 convolution_bitcast_fusion.6
  36.0 0.5 convolution_bitcast_fusion.8
  36.5 0.5 convolution_bitcast_fusion.3
  37.0 0.5 convolution_bitcast_fusion.4
  37.4 0.5 convolution_bitcast_fusion.5
  37.9 0.5 convolution_bitcast_fusion.7
  38.4 0.1 maximum_bitcast_fusion
  38.8 2.1 fusion
  40.9 0.2 fusion.20
  41.2 0.8 copy.47
  42.1 1.7 convert_bitcast_fusion
  43.7 0.2 copy-done.3
  44.0 0.3 fusion.26
  44.2 5.7 collective-permute-start.1
  49.9 0.6 multiply_convert_fusion
  50.5 0.7 convolution_bitcast_fusion.2
  51.3 8.1 %collective-permute-done.1 = bf16[2,256,512]{2,1,0:T(8,128)(2,1)S(1)} collective-permute-done((bf16[2,256,512]{2,1,0:T(8,128)(2,1)S(1)}, bf16[2,256,512]{2,1,0:T(8,128)(2,1)S(1)}, u32[]{:S(2)}, u32[]{:S(2)}) %collective-permute-start.1) | collective-permute-done | bytes 524320 | tf_op jit(solution)/shard_map/ppermute | solution.py:13
  59.3 0.2 fusion.21
  59.5 0.7 convolution_bitcast_fusion
  60.3 0.7 convolution_bitcast_fusion.1
  61.0 1.6 fusion.1
  62.7 82.9 %all-gather.2.cloned.1.call-done = bf16[8,256,3,3,512]{4,1,3,2,0:T(8,128)(2,1)} async-done(((bf16[1,256,3,3,512]{4,1,3,2,0:T(8,128)(2,1)}), bf16[8,256,3,3,512]{4,1,3,2,0:T(8,128)(2,1)}) %all-gather.2.cloned.1.call-update) | async-done | bytes 18874384 | tf_op jit(solution)/shard_map/all_gather | solution.py:108
  145.6 11.9 %reduce_sum.12 = bf16[256,3,3,512]{3,0,2,1:T(8,128)(2,1)} reduce(bf16[8,256,3,3,512]{4,1,3,2,0:T(8,128)(2,1)} %all-gather.2.cloned.1.call-done, bf16[]{:T(256)} %constant.76.clone.1), dimensions={0}, to_apply=%region_0.1 | reduce | flops 8257536 | bytes 21233666 | tf_op jit(solution)/shard_map/reduce_sum | solution.py:108
  157.6 5.3 copy.45
  162.9 7.4 %reshape.195 = bf16[256,4608]{1,0:T(8,128)(2,1)} reshape(bf16[256,3,3,512]{3,2,1,0:T(4,128)(2,1)} %copy.45) | data formatting | bytes 4718592
  170.3 1.6 fusion.35
  171.9 0.2 copy-done.4
  172.0 0.5 fusion.37
  172.5 0.5 fusion.39
  173.0 0.5 fusion.41
  173.4 0.5 fusion.44
  173.9 0.5 fusion.46
  174.4 0.5 fusion.48
  174.8 0.5 fusion.50
  175.3 0.9 fusion.14
  176.2 1.2 copy.22
  177.4 9.6 %all-to-all-start = ((bf16[1,4,256,256]{3,1,0,2:T(4,128)(2,1)}), bf16[1,4,256,256]{3,1,0,2:T(4,128)(2,1)S(1)}, u32[]{:S(2)}, u32[]{:S(2)}) async-start(bf16[1,4,256,256]{3,1,0,2:T(4,128)(2,1)} %copy.22), calls=%async_computation | async-start | bytes 1048576 | tf_op jit(solution)/shard_map/all_to_all | solution.py:103
  186.9 54.0 %reduce-scatter.12.cloned.1.call-done = bf16[16,18]{1,0:T(8,128)(2,1)} async-done(((bf16[512,18]{1,0:T(8,128)(2,1)}), bf16[16,18]{1,0:T(8,128)(2,1)}) %reduce-scatter.12.cloned.1.call-update) | async-done | bytes 592
  240.9 0.8 copy.48
  241.7 0.9 copy.23
  242.6 216.5 %reduce-scatter.8.cloned.1.call-done = bf16[16,3,512]{2,0,1:T(8,128)(2,1)} async-done(((bf16[512,3,512]{2,0,1:T(8,128)(2,1)}), bf16[16,3,512]{2,0,1:T(8,128)(2,1)}) %reduce-scatter.8.cloned.1.call-update) | async-done | bytes 49168 | tf_op jit(solution)/shard_map/reduce_scatter | solution.py:118
  459.1 27.5 %all-reduce.9 = (bf16[16,18]{0,1:T(8,128)(2,1)S(1)}, bf16[16,3,512]{2,0,1:T(8,128)(2,1)S(1)}) all-reduce(bf16[16,18]{0,1:T(8,128)(2,1)S(1)} %copy.48, bf16[16,3,512]{2,0,1:T(8,128)(2,1)} %reduce-scatter.8.cloned.1.call-done), channel_id=1, replica_groups=mesh['tm'=32,'clip'=8] {'clip'}, use_global_device_ids=true, to_apply=%region_4.5 | all-reduce | flops 24864 | bytes 99456 | tf_op jit(solution)/shard_map/psum | solution.py:112
  486.6 0.6 convert_element_type.133
  487.3 0.7 copy.25
  488.0 190.9 %reduce-scatter.10.cloned.1.call-done = bf16[8,4608]{1,0:T(8,128)(2,1)} async-done(((bf16[256,4608]{1,0:T(8,128)(2,1)}), bf16[8,4608]{1,0:T(8,128)(2,1)}) %reduce-scatter.10.cloned.1.call-update) | async-done | bytes 73744
  678.9 1.6 convert_element_type.126
  (31 shorter events, 0.7 us)
Async XLA Ops:
  8.0 4.2 copy-start
  8.0 6.2 copy-start.7
  8.0 137.6 %all-gather.2.cloned.1.call-start = ((), (), s32[]{:S(2)}) async-start(), calls=%async_computation.4 | async-start | bytes 21233664 | tf_op jit(solution)/shard_map/all_gather | solution.py:108
  12.2 3.9 copy-start.5
  14.7 13.4 %collective-permute-start = (bf16[2,256,512]{2,1,0:T(8,128)(2,1)S(1)}, bf16[2,256,512]{2,1,0:T(8,128)(2,1)S(1)}, u32[]{:S(2)}, u32[]{:S(2)}) collective-permute-start(bf16[2,256,512]{2,1,0:T(8,128)(2,1)S(1)} %bitcast.259), channel_id=1, source_target_pairs={{8,0},{16,8},{24,16},{32,24},{40,32},{48,40},{56,48},{64,56},{72,6... | collective-permute-start | bytes 1572872 | tf_op jit(solution)/shard_map/ppermute | solution.py:13
  28.3 1.2 copy-start.1
  31.9 2.3 copy-start.6
  40.9 200.0 %reduce-scatter.12.cloned.1.call-start = ((), (), s32[]{:S(2)}) async-start(), calls=%async_computation.7 | async-start | bytes 135168
  42.0 417.1 %reduce-scatter.8.cloned.1.call-start = ((), (), s32[]{:S(2)}) async-start(), calls=%async_computation.5 | async-start | bytes 1622016 | tf_op jit(solution)/shard_map/reduce_scatter | solution.py:118
  42.1 1.9 copy-start.3
  43.7 6.2 copy-start.2
  44.0 6.5 copy-start.8
  44.2 15.1 %collective-permute-start.1 = (bf16[2,256,512]{2,1,0:T(8,128)(2,1)S(1)}, bf16[2,256,512]{2,1,0:T(8,128)(2,1)S(1)}, u32[]{:S(2)}, u32[]{:S(2)}) collective-permute-start(bf16[2,256,512]{2,1,0:T(8,128)(2,1)S(1)} %bitcast.257), channel_id=1, source_target_pairs={{0,8},{8,16},{16,24},{24,32},{32,40},{40,48},{48,56},{56,64},{64,7... | collective-permute-start | bytes 1572872 | tf_op jit(solution)/shard_map/ppermute | solution.py:13
  62.6 616.2 %reduce-scatter.10.cloned.1.call-start = ((), (), s32[]{:S(2)}) async-start(), calls=%async_computation.6 | async-start | bytes 2433024
  170.3 1.8 copy-start.4
  177.4 64.3 %all-to-all-start = ((bf16[1,4,256,256]{3,1,0,2:T(4,128)(2,1)}), bf16[1,4,256,256]{3,1,0,2:T(4,128)(2,1)S(1)}, u32[]{:S(2)}, u32[]{:S(2)}) async-start(bf16[1,4,256,256]{3,1,0,2:T(4,128)(2,1)} %copy.22), calls=%async_computation | async-start | bytes 1048576 | tf_op jit(solution)/shard_map/all_to_all | solution.py:103
Sparse Core Ops, SparseCore 0:
  41.0 104.5 all-gather.1
Sparse Core Ops, SparseCore 1:
  45.6 195.3 reduce-scatter.11
  245.1 214.0 reduce-scatter.7
  463.3 215.5 reduce-scatter.9
